TPU v7x, 32 devices: a whole 2x2x4 slice. The times are simulated.
32 devices in a mesh: grp: 2 (over x), seq: 8 (over z, y), head: 2 (over core).
Axes of the slice: x: 2, y: 2, z: 4, core: 2. Of those that a mesh axis runs over, the one named last changes fastest.
Arguments:
- queries: bfloat16 [16384, 2048], P(('grp', 'seq'), 'head'), parts along dimension 0, may hold values from -6 to 6
- key_states: bfloat16 [16384, 1024], P(('grp', 'seq'), 'head'), parts along dimension 0, may hold values from -6 to 6
- value_states: bfloat16 [16384, 1024], P(('grp', 'seq'), 'head'), parts along dimension 0, may hold values from -6 to 6
- segment_ids: int32 [16384], P(('grp', 'seq')), parts along dimension 0, may hold values from 0 to 15, as said below
Outputs:
- attended: bfloat16 [16384, 2048], P(('grp', 'seq'), 'head'), parts along dimension 0
There are 2 independent parts, one for each index of `grp`. A program takes and returns all parts, laid end to end along the dimension named above; each array names one. Nothing has to cross between parts.
Inputs may be any that keep to these rules, and one draw needn't show every extreme that they name: `segment_ids`: read in logical order, the ids never fall, start at 0 and name all 16 candidates, each one token or more; the first 1536 and the last 1536 logical tokens each lie within one candidate.
All inputs are finite; a program needn't handle non-finite values.
Results may differ from a plain program's by a relative error of at most 0.008.
Values may be sent and summed in bfloat16 or wider, within the bound.
A program may use at most 64 MiB of HBM per device.

v0:
```python
import jax
import jax.numpy as jnp
from jax import lax
from jax.sharding import PartitionSpec as P

HEAD_DIM = 128
WINDOW = 1024


attn_scale = 168.0 ** (-0.5)


def passed_along(block, axis, distance):
    devices = range(lax.axis_size(axis))
    route = [(i - distance, i) for i in devices if i - distance in devices]
    return lax.ppermute(block, axis, route)


def attend_block(query_blk, key_band, value_band, query_seg, key_seg, query_pos, key_pos):
    row_count = query_blk.shape[0]
    key_count = key_band.shape[0]
    kv_heads = key_band.shape[1] // HEAD_DIM
    groups = query_blk.shape[1] // key_band.shape[1]
    query_heads = query_blk.reshape(row_count, kv_heads, groups, HEAD_DIM).transpose(1, 0, 2, 3)
    key_heads = key_band.reshape(key_count, kv_heads, HEAD_DIM).transpose(1, 0, 2)
    value_heads = value_band.reshape(key_count, kv_heads, HEAD_DIM).transpose(1, 0, 2)
    visible = (key_pos[None, :] <= query_pos[:, None]) & (
        key_pos[None, :] > query_pos[:, None] - WINDOW
    )
    visible = visible & (key_pos[None, :] >= 0) & (key_seg[None, :] == query_seg[:, None])

    def one_head(operands):
        query_one, key_one, value_one = operands
        scores = (
            jnp.einsum("qgd,kd->gqk", query_one, key_one, preferred_element_type=jnp.float32)
            * attn_scale
        )
        scores = jnp.where(visible[None], scores, jnp.float32(-1e30))
        row_max = jnp.max(scores, axis=-1, keepdims=True)
        exp_terms = jnp.exp(scores - row_max)
        weights = (exp_terms / jnp.sum(exp_terms, axis=-1, keepdims=True)).astype(jnp.bfloat16)
        return jnp.einsum(
            "gqk,kd->qgd", weights, value_one, preferred_element_type=jnp.float32
        ).astype(jnp.bfloat16)

    mixed_out = lax.map(one_head, (query_heads, key_heads, value_heads))
    return mixed_out.transpose(1, 0, 2, 3).reshape(row_count, query_blk.shape[1])


def pick_rows(condition, first_set, second_set):
    return tuple(
        (
            jnp.where(condition, first_one, second_one)
            for first_one, second_one in zip(first_set, second_set)
        )
    )


def join_band(older_set, middle_set, latest_set):
    return tuple(
        (
            jnp.concatenate([older, middle, latest], axis=0)
            for older, middle, latest in zip(older_set, middle_set, latest_set)
        )
    )


def body(queries, key_states, value_states, segment_ids):
    half_rows = queries.shape[0] // 2
    seq_count = lax.axis_size("seq")
    seq_index = lax.axis_index("seq")
    key_front = key_states[:half_rows]
    value_front = value_states[:half_rows]
    seg_front = segment_ids[:half_rows]
    key_back = key_states[half_rows:]
    value_back = value_states[half_rows:]
    seg_back = segment_ids[half_rows:]
    front_part = (key_front, value_front, seg_front)
    back_part = (key_back, value_back, seg_back)
    prev_first = passed_along((key_front, value_front, seg_front), "seq", 1)
    prev_second = passed_along((key_front, value_front, seg_front), "seq", 2)
    next_first = passed_along(
        (key_back, value_back, seg_back, key_front, value_front, seg_front), "seq", -1
    )
    next_back = (next_first[0], next_first[1], next_first[2])
    next_front = (next_first[3], next_first[4], next_first[5])
    next_second = passed_along((key_back, value_back, seg_back), "seq", -2)
    is_last = seq_index == seq_count - 1
    is_second = seq_index == seq_count - 2
    back_one = pick_rows(is_last, front_part, next_back)
    back_two = pick_rows(is_last, prev_first, pick_rows(is_second, next_front, next_second))
    band_front = join_band(prev_second, prev_first, front_part)
    band_back = join_band(back_two, back_one, back_part)
    local_pos = jnp.arange(half_rows, dtype=jnp.int32)
    band_pos = jnp.arange(3 * half_rows, dtype=jnp.int32)
    front_start = seq_index * half_rows
    back_start = (2 * seq_count - 1 - seq_index) * half_rows
    out_front = attend_block(
        queries[:half_rows],
        band_front[0],
        band_front[1],
        seg_front,
        band_front[2],
        front_start + local_pos,
        front_start - 2 * half_rows + band_pos,
    )
    out_back = attend_block(
        queries[half_rows:],
        band_back[0],
        band_back[1],
        seg_back,
        band_back[2],
        back_start + local_pos,
        back_start - 2 * half_rows + band_pos,
    )
    return jnp.concatenate([out_front, out_back], axis=0)


def solution(mesh):
    in_specs = (
        P(("grp", "seq"), "head"),
        P(("grp", "seq"), "head"),
        P(("grp", "seq"), "head"),
        P(("grp", "seq")),
    )
    out_specs = P(("grp", "seq"), "head")
    return jax.shard_map(body, mesh=mesh, in_specs=in_specs, out_specs=out_specs, check_vma=False)
```

profile of v0, /device:TPU:0, one launch (start us, length us, event | category | flops | bytes accessed | tf_op | source)
XLA Modules:
  0.0 184.1 jit_solution(14074200972316602542)
XLA Ops:
  7.2 6.9 %collective-permute-start.1 = (bf16[512,512]{0,1:T(8,128)(2,1)S(1)}, bf16[512,512]{0,1:T(8,128)(2,1)}, u32[]{:S(2)}, u32[]{:S(2)}) collective-permute-start(bf16[512,512]{0,1:T(8,128)(2,1)S(1)} %copy.33), channel_id=1, source_target_pairs={{0,2},{2,4},{4,6},{6,8},{8,10},{10,12},{12,14},{1,3},{3,5},{5,7},{... | collective-permute-start | bytes 1572872 | tf_op jit(solution)/shard_map/ppermute | solution.py:16
  16.8 4.7 %collective-permute-start.3 = (s32[512]{0:T(512)S(1)}, s32[512]{0:T(512)S(1)}, u32[]{:S(2)}, u32[]{:S(2)}) collective-permute-start(s32[512]{0:T(512)S(1)} %get-tuple-element.388), channel_id=1, source_target_pairs={{0,2},{2,4},{4,6},{6,8},{8,10},{10,12},{12,14},{1,3},{3,5},{5,7},{... | collective-permute-start | bytes 6152 | tf_op jit(solution)/shard_map/ppermute | solution.py:16
  29.1 17.6 %collective-permute-done.3 = s32[512]{0:T(512)S(1)} collective-permute-done((s32[512]{0:T(512)S(1)}, s32[512]{0:T(512)S(1)}, u32[]{:S(2)}, u32[]{:S(2)}) %collective-permute-start.3) | collective-permute-done | bytes 2080 | tf_op jit(solution)/shard_map/ppermute | solution.py:16
  48.0 4.5 %collective-permute-start.2 = (s32[512]{0:T(512)S(1)}, s32[512]{0:T(512)S(1)}, u32[]{:S(2)}, u32[]{:S(2)}) collective-permute-start(s32[512]{0:T(512)S(1)} %get-tuple-element.388), channel_id=1, source_target_pairs={{0,4},{2,6},{4,8},{6,10},{8,12},{10,14},{1,5},{3,7},{5,9},{7,11},{... | collective-permute-start | bytes 6152 | tf_op jit(solution)/shard_map/ppermute | solution.py:16
  55.1 5.1 %collective-permute-start.5 = (bf16[512,512]{0,1:T(8,128)(2,1)S(1)}, bf16[512,512]{0,1:T(8,128)(2,1)S(1)}, u32[]{:S(2)}, u32[]{:S(2)}) collective-permute-start(bf16[512,512]{0,1:T(8,128)(2,1)S(1)} %copy.34), channel_id=1, source_target_pairs={{0,2},{2,4},{4,6},{6,8},{8,10},{10,12},{12,14},{1,3},{3,5},{5,7},{... | collective-permute-start | bytes 1572872 | tf_op jit(solution)/shard_map/ppermute | solution.py:16
  64.0 8.3 %collective-permute-start = (bf16[512,512]{0,1:T(8,128)(2,1)S(1)}, bf16[512,512]{0,1:T(8,128)(2,1)}, u32[]{:S(2)}, u32[]{:S(2)}) collective-permute-start(bf16[512,512]{0,1:T(8,128)(2,1)S(1)} %copy.33), channel_id=1, source_target_pairs={{0,4},{2,6},{4,8},{6,10},{8,12},{10,14},{1,5},{3,7},{5,9},{7,11},{... | collective-permute-start | bytes 1572872 | tf_op jit(solution)/shard_map/ppermute | solution.py:16
  72.4 14.9 %collective-permute-start.4 = (bf16[512,512]{0,1:T(8,128)(2,1)S(1)}, bf16[512,512]{0,1:T(8,128)(2,1)}, u32[]{:S(2)}, u32[]{:S(2)}) collective-permute-start(bf16[512,512]{0,1:T(8,128)(2,1)S(1)} %copy.34), channel_id=1, source_target_pairs={{0,4},{2,6},{4,8},{6,10},{8,12},{10,14},{1,5},{3,7},{5,9},{7,11},{... | collective-permute-start | bytes 1572872 | tf_op jit(solution)/shard_map/ppermute | solution.py:16
  97.9 37.9 %while.23 = (s32[]{:T(128)}, bf16[4,512,2,128]{1,3,2,0:T(8,128)(2,1)S(1)}, bf16[4,1536,128]{1,2,0:T(8,128)(2,1)}, bf16[4,1536,128]{1,2,0:T(8,128)(2,1)}, bf16[4,...) while((s32[]{:T(128)}, ...), condition=%wide.region_7.8_spmd.clone, body=%wide.region_4.7_spmd.clone.sunk | while | flops 1226969088 | bytes 4356733 | solution.py:46
  99.4 3.6 %fusion.142 = f32[2,512]{1,0:T(2,128)S(1)} fusion(pred[512,1536]{0,1:T(8,128)(4,1)S(1)} %compare_and_fusion.5, bf16[4,1536,128]{1,2,0:T(8,128)(2,1)} %get-tuple-element.370, s32[]{:T(128)S(6)} %copy.43, bf16[4,512,2,128]{1,3,2,0:T(8,128)(2,1)} %get-tuple-element.371), kind=kOutput, calls=%fused_computation.90.clone.1 | convolution fusion | flops 408946176 | bytes 1446912 | tf_op jit(solution)/shard_map/while/body/eval_jaxpr/sub | solution.py:40
  103.0 4.3 %fusion.143 = bf16[4,512,2,128]{1,3,2,0:T(8,128)(2,1)S(1)} fusion(bf16[4,512,2,128]{1,3,2,0:T(8,128)(2,1)S(1)} %get-tuple-element.356, s32[]{:T(128)S(6)} %copy.43, f32[2,512]{1,0:T(2,128)S(1)} %fusion.142, bf16[4,1536,128]{1,2,0:T(8,128)(2,1)} %get-tuple-element.369, pred[512,1536]{0,1:T(8,128)(4,1)S(1)} %compare_and_fusion.5, ...), kind=kOutput, calls=%fused_computation.47.clone.1 | convolution fusion | flops 813304320 | bytes 2103296 | tf_op jit(solution)/shard_map/while/body/eval_jaxpr/gqk,kd->qgd/dot_general | solution.py:42
  108.9 3.6 %fusion.142 = f32[2,512]{1,0:T(2,128)S(1)} fusion(pred[512,1536]{0,1:T(8,128)(4,1)S(1)} %compare_and_fusion.5, bf16[4,1536,128]{1,2,0:T(8,128)(2,1)} %get-tuple-element.370, s32[]{:T(128)S(6)} %copy.43, bf16[4,512,2,128]{1,3,2,0:T(8,128)(2,1)} %get-tuple-element.371), kind=kOutput, calls=%fused_computation.90.clone.1 | convolution fusion | flops 408946176 | bytes 1446912 | tf_op jit(solution)/shard_map/while/body/eval_jaxpr/sub | solution.py:40
  112.5 4.3 %fusion.143 = bf16[4,512,2,128]{1,3,2,0:T(8,128)(2,1)S(1)} fusion(bf16[4,512,2,128]{1,3,2,0:T(8,128)(2,1)S(1)} %get-tuple-element.356, s32[]{:T(128)S(6)} %copy.43, f32[2,512]{1,0:T(2,128)S(1)} %fusion.142, bf16[4,1536,128]{1,2,0:T(8,128)(2,1)} %get-tuple-element.369, pred[512,1536]{0,1:T(8,128)(4,1)S(1)} %compare_and_fusion.5, ...), kind=kOutput, calls=%fused_computation.47.clone.1 | convolution fusion | flops 813304320 | bytes 2103296 | tf_op jit(solution)/shard_map/while/body/eval_jaxpr/gqk,kd->qgd/dot_general | solution.py:42
  118.4 3.6 %fusion.142 = f32[2,512]{1,0:T(2,128)S(1)} fusion(pred[512,1536]{0,1:T(8,128)(4,1)S(1)} %compare_and_fusion.5, bf16[4,1536,128]{1,2,0:T(8,128)(2,1)} %get-tuple-element.370, s32[]{:T(128)S(6)} %copy.43, bf16[4,512,2,128]{1,3,2,0:T(8,128)(2,1)} %get-tuple-element.371), kind=kOutput, calls=%fused_computation.90.clone.1 | convolution fusion | flops 408946176 | bytes 1446912 | tf_op jit(solution)/shard_map/while/body/eval_jaxpr/sub | solution.py:40
  122.0 4.3 %fusion.143 = bf16[4,512,2,128]{1,3,2,0:T(8,128)(2,1)S(1)} fusion(bf16[4,512,2,128]{1,3,2,0:T(8,128)(2,1)S(1)} %get-tuple-element.356, s32[]{:T(128)S(6)} %copy.43, f32[2,512]{1,0:T(2,128)S(1)} %fusion.142, bf16[4,1536,128]{1,2,0:T(8,128)(2,1)} %get-tuple-element.369, pred[512,1536]{0,1:T(8,128)(4,1)S(1)} %compare_and_fusion.5, ...), kind=kOutput, calls=%fused_computation.47.clone.1 | convolution fusion | flops 813304320 | bytes 2103296 | tf_op jit(solution)/shard_map/while/body/eval_jaxpr/gqk,kd->qgd/dot_general | solution.py:42
  127.9 3.6 %fusion.142 = f32[2,512]{1,0:T(2,128)S(1)} fusion(pred[512,1536]{0,1:T(8,128)(4,1)S(1)} %compare_and_fusion.5, bf16[4,1536,128]{1,2,0:T(8,128)(2,1)} %get-tuple-element.370, s32[]{:T(128)S(6)} %copy.43, bf16[4,512,2,128]{1,3,2,0:T(8,128)(2,1)} %get-tuple-element.371), kind=kOutput, calls=%fused_computation.90.clone.1 | convolution fusion | flops 408946176 | bytes 1446912 | tf_op jit(solution)/shard_map/while/body/eval_jaxpr/sub | solution.py:40
  131.5 4.3 %fusion.143 = bf16[4,512,2,128]{1,3,2,0:T(8,128)(2,1)S(1)} fusion(bf16[4,512,2,128]{1,3,2,0:T(8,128)(2,1)S(1)} %get-tuple-element.356, s32[]{:T(128)S(6)} %copy.43, f32[2,512]{1,0:T(2,128)S(1)} %fusion.142, bf16[4,1536,128]{1,2,0:T(8,128)(2,1)} %get-tuple-element.369, pred[512,1536]{0,1:T(8,128)(4,1)S(1)} %compare_and_fusion.5, ...), kind=kOutput, calls=%fused_computation.47.clone.1 | convolution fusion | flops 813304320 | bytes 2103296 | tf_op jit(solution)/shard_map/while/body/eval_jaxpr/gqk,kd->qgd/dot_general | solution.py:42
  142.0 38.1 %while.22 = (s32[]{:T(128)}, bf16[4,512,2,128]{1,3,2,0:T(8,128)(2,1)S(1)}, bf16[4,1536,128]{1,2,0:T(8,128)(2,1)}, bf16[4,1536,128]{1,2,0:T(8,128)(2,1)}, bf16[4,...) while((s32[]{:T(128)}, ...), condition=%wide.region_3.4_spmd.clone, body=%wide.region_0.3_spmd.clone.sunk | while | flops 1226969088 | bytes 4356733 | solution.py:46
  143.7 3.6 %fusion.135 = f32[2,512]{1,0:T(2,128)S(1)} fusion(pred[512,1536]{0,1:T(8,128)(4,1)S(1)} %compare_and_fusion.4, bf16[4,1536,128]{1,2,0:T(8,128)(2,1)} %get-tuple-element.406, s32[]{:T(128)S(6)} %copy.49, bf16[4,512,2,128]{1,3,2,0:T(8,128)(2,1)} %get-tuple-element.407), kind=kOutput, calls=%fused_computation.89.clone.1 | convolution fusion | flops 408946176 | bytes 1446912 | tf_op jit(solution)/shard_map/while/body/eval_jaxpr/sub | solution.py:40
  147.3 4.3 %fusion.136 = bf16[4,512,2,128]{1,3,2,0:T(8,128)(2,1)S(1)} fusion(bf16[4,512,2,128]{1,3,2,0:T(8,128)(2,1)S(1)} %get-tuple-element.392, s32[]{:T(128)S(6)} %copy.49, f32[2,512]{1,0:T(2,128)S(1)} %fusion.135, bf16[4,1536,128]{1,2,0:T(8,128)(2,1)} %get-tuple-element.405, pred[512,1536]{0,1:T(8,128)(4,1)S(1)} %compare_and_fusion.4, ...), kind=kOutput, calls=%fused_computation.14.clone.1 | convolution fusion | flops 813304320 | bytes 2103296 | tf_op jit(solution)/shard_map/while/body/eval_jaxpr/gqk,kd->qgd/dot_general | solution.py:42
  153.2 3.6 %fusion.135 = f32[2,512]{1,0:T(2,128)S(1)} fusion(pred[512,1536]{0,1:T(8,128)(4,1)S(1)} %compare_and_fusion.4, bf16[4,1536,128]{1,2,0:T(8,128)(2,1)} %get-tuple-element.406, s32[]{:T(128)S(6)} %copy.49, bf16[4,512,2,128]{1,3,2,0:T(8,128)(2,1)} %get-tuple-element.407), kind=kOutput, calls=%fused_computation.89.clone.1 | convolution fusion | flops 408946176 | bytes 1446912 | tf_op jit(solution)/shard_map/while/body/eval_jaxpr/sub | solution.py:40
  156.8 4.3 %fusion.136 = bf16[4,512,2,128]{1,3,2,0:T(8,128)(2,1)S(1)} fusion(bf16[4,512,2,128]{1,3,2,0:T(8,128)(2,1)S(1)} %get-tuple-element.392, s32[]{:T(128)S(6)} %copy.49, f32[2,512]{1,0:T(2,128)S(1)} %fusion.135, bf16[4,1536,128]{1,2,0:T(8,128)(2,1)} %get-tuple-element.405, pred[512,1536]{0,1:T(8,128)(4,1)S(1)} %compare_and_fusion.4, ...), kind=kOutput, calls=%fused_computation.14.clone.1 | convolution fusion | flops 813304320 | bytes 2103296 | tf_op jit(solution)/shard_map/while/body/eval_jaxpr/gqk,kd->qgd/dot_general | solution.py:42
  166.2 4.3 %fusion.136 = bf16[4,512,2,128]{1,3,2,0:T(8,128)(2,1)S(1)} fusion(bf16[4,512,2,128]{1,3,2,0:T(8,128)(2,1)S(1)} %get-tuple-element.392, s32[]{:T(128)S(6)} %copy.49, f32[2,512]{1,0:T(2,128)S(1)} %fusion.135, bf16[4,1536,128]{1,2,0:T(8,128)(2,1)} %get-tuple-element.405, pred[512,1536]{0,1:T(8,128)(4,1)S(1)} %compare_and_fusion.4, ...), kind=kOutput, calls=%fused_computation.14.clone.1 | convolution fusion | flops 813304320 | bytes 2103296 | tf_op jit(solution)/shard_map/while/body/eval_jaxpr/gqk,kd->qgd/dot_general | solution.py:42
  172.2 3.6 %fusion.135 = f32[2,512]{1,0:T(2,128)S(1)} fusion(pred[512,1536]{0,1:T(8,128)(4,1)S(1)} %compare_and_fusion.4, bf16[4,1536,128]{1,2,0:T(8,128)(2,1)} %get-tuple-element.406, s32[]{:T(128)S(6)} %copy.49, bf16[4,512,2,128]{1,3,2,0:T(8,128)(2,1)} %get-tuple-element.407), kind=kOutput, calls=%fused_computation.89.clone.1 | convolution fusion | flops 408946176 | bytes 1446912 | tf_op jit(solution)/shard_map/while/body/eval_jaxpr/sub | solution.py:40
  175.7 4.3 %fusion.136 = bf16[4,512,2,128]{1,3,2,0:T(8,128)(2,1)S(1)} fusion(bf16[4,512,2,128]{1,3,2,0:T(8,128)(2,1)S(1)} %get-tuple-element.392, s32[]{:T(128)S(6)} %copy.49, f32[2,512]{1,0:T(2,128)S(1)} %fusion.135, bf16[4,1536,128]{1,2,0:T(8,128)(2,1)} %get-tuple-element.405, pred[512,1536]{0,1:T(8,128)(4,1)S(1)} %compare_and_fusion.4, ...), kind=kOutput, calls=%fused_computation.14.clone.1 | convolution fusion | flops 813304320 | bytes 2103296 | tf_op jit(solution)/shard_map/while/body/eval_jaxpr/gqk,kd->qgd/dot_general | solution.py:42
  (73 shorter events, 61.6 us)
Async XLA Ops:
  0.7 13.4 %copy-start.2 = (bf16[1024,512]{1,0:T(8,128)(2,1)S(1)}, bf16[1024,512]{1,0:T(8,128)(2,1)}, u32[]{:S(2)}) copy-start(bf16[1024,512]{1,0:T(8,128)(2,1)} %param.9) | copy-start | bytes 3145732
  0.7 16.1 %collective-permute-start.11 = (s32[512]{0:T(512)S(1)}, s32[512]{0:T(512)S(1)}, u32[]{:S(2)}, u32[]{:S(2)}) collective-permute-start(s32[512]{0:T(512)S(1)} %slice.29), channel_id=1, source_target_pairs={{2,0},{4,2},{6,4},{8,6},{10,8},{12,10},{14,12},{3,1},{5,3},{7,5},{... | collective-permute-start | bytes 6152 | tf_op jit(solution)/shard_map/ppermute | solution.py:16
  2.1 25.7 %collective-permute-start.10 = (s32[512]{0:T(512)S(1)}, s32[512]{0:T(512)S(1)}, u32[]{:S(2)}, u32[]{:S(2)}) collective-permute-start(s32[512]{0:T(512)S(1)} %slice.29), channel_id=1, source_target_pairs={{4,0},{6,2},{8,4},{10,6},{12,8},{14,10},{5,1},{7,3},{9,5},{11,7},{... | collective-permute-start | bytes 6152 | tf_op jit(solution)/shard_map/ppermute | solution.py:16
  5.7 49.4 %collective-permute-start.8 = (bf16[512,512]{0,1:T(8,128)(2,1)}, bf16[512,512]{0,1:T(8,128)(2,1)}, u32[]{:S(2)}, u32[]{:S(2)}) collective-permute-start(bf16[512,512]{0,1:T(8,128)(2,1)} %copy.36), channel_id=1, source_target_pairs={{2,0},{4,2},{6,4},{8,6},{10,8},{12,10},{14,12},{3,1},{5,3},{7,5},{... | collective-permute-start | bytes 1572872 | tf_op jit(solution)/shard_map/ppermute | solution.py:16
  7.2 54.2 %collective-permute-start.1 = (bf16[512,512]{0,1:T(8,128)(2,1)S(1)}, bf16[512,512]{0,1:T(8,128)(2,1)}, u32[]{:S(2)}, u32[]{:S(2)}) collective-permute-start(bf16[512,512]{0,1:T(8,128)(2,1)S(1)} %copy.33), channel_id=1, source_target_pairs={{0,2},{2,4},{4,6},{6,8},{8,10},{10,12},{12,14},{1,3},{3,5},{5,7},{... | collective-permute-start | bytes 1572872 | tf_op jit(solution)/shard_map/ppermute | solution.py:16
  15.0 1.8 copy-start.3
  16.8 29.8 %collective-permute-start.3 = (s32[512]{0:T(512)S(1)}, s32[512]{0:T(512)S(1)}, u32[]{:S(2)}, u32[]{:S(2)}) collective-permute-start(s32[512]{0:T(512)S(1)} %get-tuple-element.388), channel_id=1, source_target_pairs={{0,2},{2,4},{4,6},{6,8},{8,10},{10,12},{12,14},{1,3},{3,5},{5,7},{... | collective-permute-start | bytes 6152 | tf_op jit(solution)/shard_map/ppermute | solution.py:16
  21.5 26.4 %collective-permute-start.9 = (s32[512]{0:T(512)S(1)}, s32[512]{0:T(512)S(1)}, u32[]{:S(2)}, u32[]{:S(2)}) collective-permute-start(s32[512]{0:T(512)S(1)} %get-tuple-element.388), channel_id=1, source_target_pairs={{2,0},{4,2},{6,4},{8,6},{10,8},{12,10},{14,12},{3,1},{5,3},{7,5},{... | collective-permute-start | bytes 6152 | tf_op jit(solution)/shard_map/ppermute | solution.py:16
  26.5 27.4 %copy-start.1 = (bf16[512,512]{0,1:T(8,128)(2,1)S(1)}, bf16[512,512]{0,1:T(8,128)(2,1)}, u32[]{:S(2)}) copy-start(bf16[512,512]{0,1:T(8,128)(2,1)} %copy.37) | copy-start | bytes 1572868
  27.8 34.9 %collective-permute-start.6 = (bf16[512,512]{0,1:T(8,128)(2,1)S(1)}, bf16[512,512]{0,1:T(8,128)(2,1)S(1)}, u32[]{:S(2)}, u32[]{:S(2)}) collective-permute-start(bf16[512,512]{0,1:T(8,128)(2,1)S(1)} %copy.33), channel_id=1, source_target_pairs={{2,0},{4,2},{6,4},{8,6},{10,8},{12,10},{14,12},{3,1},{5,3},{7,5},{... | collective-permute-start | bytes 1572872 | tf_op jit(solution)/shard_map/ppermute | solution.py:16
  46.7 17.3 %collective-permute-start.7 = (bf16[512,512]{0,1:T(8,128)(2,1)}, bf16[512,512]{0,1:T(8,128)(2,1)S(1)}, u32[]{:S(2)}, u32[]{:S(2)}) collective-permute-start(bf16[512,512]{0,1:T(8,128)(2,1)} %copy.36), channel_id=1, source_target_pairs={{4,0},{6,2},{8,4},{10,6},{12,8},{14,10},{5,1},{7,3},{9,5},{11,7},{... | collective-permute-start | bytes 1572872 | tf_op jit(solution)/shard_map/ppermute | solution.py:16
  48.0 5.8 %collective-permute-start.2 = (s32[512]{0:T(512)S(1)}, s32[512]{0:T(512)S(1)}, u32[]{:S(2)}, u32[]{:S(2)}) collective-permute-start(s32[512]{0:T(512)S(1)} %get-tuple-element.388), channel_id=1, source_target_pairs={{0,4},{2,6},{4,8},{6,10},{8,12},{10,14},{1,5},{3,7},{5,9},{7,11},{... | collective-permute-start | bytes 6152 | tf_op jit(solution)/shard_map/ppermute | solution.py:16
  53.8 18.6 %collective-permute-start.14 = (bf16[512,512]{0,1:T(8,128)(2,1)S(1)}, bf16[512,512]{0,1:T(8,128)(2,1)S(1)}, u32[]{:S(2)}, u32[]{:S(2)}) collective-permute-start(bf16[512,512]{0,1:T(8,128)(2,1)S(1)} %copy-done.1), channel_id=1, source_target_pairs={{2,0},{4,2},{6,4},{8,6},{10,8},{12,10},{14,12},{3,1},{5,3},{7,5},{... | collective-permute-start | bytes 1572872 | tf_op jit(solution)/shard_map/ppermute | solution.py:16
  55.1 37.9 %collective-permute-start.5 = (bf16[512,512]{0,1:T(8,128)(2,1)S(1)}, bf16[512,512]{0,1:T(8,128)(2,1)S(1)}, u32[]{:S(2)}, u32[]{:S(2)}) collective-permute-start(bf16[512,512]{0,1:T(8,128)(2,1)S(1)} %copy.34), channel_id=1, source_target_pairs={{0,2},{2,4},{4,6},{6,8},{8,10},{10,12},{12,14},{1,3},{3,5},{5,7},{... | collective-permute-start | bytes 1572872 | tf_op jit(solution)/shard_map/ppermute | solution.py:16
  61.4 31.6 %collective-permute-start.12 = (bf16[512,512]{0,1:T(8,128)(2,1)S(1)}, bf16[512,512]{0,1:T(8,128)(2,1)S(1)}, u32[]{:S(2)}, u32[]{:S(2)}) collective-permute-start(bf16[512,512]{0,1:T(8,128)(2,1)S(1)} %copy.34), channel_id=1, source_target_pairs={{2,0},{4,2},{6,4},{8,6},{10,8},{12,10},{14,12},{3,1},{5,3},{7,5},{... | collective-permute-start | bytes 1572872 | tf_op jit(solution)/shard_map/ppermute | solution.py:16
  62.7 33.7 %collective-permute-start.13 = (bf16[512,512]{0,1:T(8,128)(2,1)S(1)}, bf16[512,512]{0,1:T(8,128)(2,1)S(1)}, u32[]{:S(2)}, u32[]{:S(2)}) collective-permute-start(bf16[512,512]{0,1:T(8,128)(2,1)S(1)} %copy-done.1), channel_id=1, source_target_pairs={{4,0},{6,2},{8,4},{10,6},{12,8},{14,10},{5,1},{7,3},{9,5},{11,7},{... | collective-permute-start | bytes 1572872 | tf_op jit(solution)/shard_map/ppermute | solution.py:16
  64.0 73.1 %collective-permute-start = (bf16[512,512]{0,1:T(8,128)(2,1)S(1)}, bf16[512,512]{0,1:T(8,128)(2,1)}, u32[]{:S(2)}, u32[]{:S(2)}) collective-permute-start(bf16[512,512]{0,1:T(8,128)(2,1)S(1)} %copy.33), channel_id=1, source_target_pairs={{0,4},{2,6},{4,8},{6,10},{8,12},{10,14},{1,5},{3,7},{5,9},{7,11},{... | collective-permute-start | bytes 1572872 | tf_op jit(solution)/shard_map/ppermute | solution.py:16
  72.4 67.2 %collective-permute-start.4 = (bf16[512,512]{0,1:T(8,128)(2,1)S(1)}, bf16[512,512]{0,1:T(8,128)(2,1)}, u32[]{:S(2)}, u32[]{:S(2)}) collective-permute-start(bf16[512,512]{0,1:T(8,128)(2,1)S(1)} %copy.34), channel_id=1, source_target_pairs={{0,4},{2,6},{4,8},{6,10},{8,12},{10,14},{1,5},{3,7},{5,9},{7,11},{... | collective-permute-start | bytes 1572872 | tf_op jit(solution)/shard_map/ppermute | solution.py:16
  180.1 1.3 copy-start
where the time goes:
time: 185 us; the launch traced here: 184 us
  matrix products  63.2 us (34%)
  starting transfers between devices  56.2 us (30%)
  waiting for transfers between devices  25.6 us (14%)
  other arithmetic  24.8 us (13%)
  local copies, waits for them, and re-layouts  13.5 us (7%)
    ppermute x15, starting transfers between devices, passed_along(): return lax.ppermute(block, axis, route)  56.2 us
    dot_general x8, matrix products, one_head(): jnp.einsum('gqk,kd->qgd', weights, value_one, preferred_element_type=jnp....  34.7 us
    sub x8, matrix products, one_head(): exp_terms = jnp.exp(scores - row_max)  28.5 us
    ppermute x15, waiting for transfers between devices, passed_along(): return lax.ppermute(block, axis, route)  25.6 us
    and x8, other arithmetic, attend_block(): visible & (key_pos[None, :] >= 0) & (key_seg[None, :] == query_seg[:, None])  12.4 us
    concatenate x6, other arithmetic, join_band(): jnp.concatenate([older, middle, latest], axis=0)  8.28 us
    unnamed x14, local copies, waits for them, and re-layouts  6.18 us
  transfers between devices with their start and end apart: 15, of which 4 were waited for; matrix products, arithmetic and copies ran while one was open for 31% of the time, Pallas kernels for 0%

commit v1 on v0

v1 whole, which is shorter than its diff:
```python
import functools

import jax
import jax.numpy as jnp
from jax import lax
from jax.experimental import pallas as pl
from jax.experimental.pallas import tpu as pltpu
from jax.sharding import PartitionSpec as P

HEAD_DIM = 128
WINDOW = 1024
LANES = 128
TILE = 256
MESH = pl.DeviceIdType.MESH

SCALE2 = (168.0 ** (-0.5)) * 1.4426950408889634
NEG = -1e30

OWN_F, OWN_B, FP1, FP2, BN1, BN2 = range(6)


def kernel(n, kv_heads, groups, q_hbm, k_hbm, v_hbm, seg_ref, o_hbm,
           kv, q_vm, o_vm, segs, lo,
           send_sem, recv_sem, seg_send, seg_recv, own_sem, q_sem, o_sem):
    me = lax.axis_index("seq")
    half = q_vm.shape[0] // 2
    rows_seg = half // LANES

    offsets = (1, 2, -1, -2)
    slots = (FP1, FP2, BN1, BN2)

    def exists(off):
        return (me + off >= 0) & (me + off < n)

    barrier = pltpu.get_barrier_semaphore()
    for off in offsets:
        @pl.when(exists(off))
        def _():
            pl.semaphore_signal(barrier, inc=1, device_id={"seq": me + off}, device_id_type=MESH)
    peers = sum(exists(off).astype(jnp.int32) for off in offsets)
    pl.semaphore_wait(barrier, peers)

    def seg_copy(j):
        return pltpu.make_async_remote_copy(
            src_ref=seg_ref, dst_ref=segs.at[j], send_sem=seg_send.at[j], recv_sem=seg_recv.at[j],
            device_id={"seq": me + offsets[j]}, device_id_type=MESH)

    def part(ref, row, h):
        return ref.at[pl.ds(row, half), pl.ds(pl.multiple_of(h * HEAD_DIM, HEAD_DIM), HEAD_DIM)]

    def kv_copy(j, which, h, off=None, row=None):
        off = offsets[j] if off is None else off
        row = (0 if j < 2 else half) if row is None else row
        return pltpu.make_async_remote_copy(
            src_ref=part((k_hbm, v_hbm)[which], row, h), dst_ref=kv.at[slots[j], which, h],
            send_sem=send_sem.at[j, which, h], recv_sem=recv_sem.at[j, which, h],
            device_id={"seq": me + off}, device_id_type=MESH)

    def edge_copy(which, h):
        return pltpu.make_async_remote_copy(
            src_ref=part((k_hbm, v_hbm)[which], 0, h), dst_ref=kv.at[BN2, which, h],
            send_sem=send_sem.at[4, which, h], recv_sem=recv_sem.at[3, which, h],
            device_id={"seq": me - 1}, device_id_type=MESH)

    def start_sends(h):
        for j in range(4):
            @pl.when(exists(offsets[j]))
            def _():
                for which in range(2):
                    kv_copy(j, which, h).start()

        @pl.when(me == n - 1)
        def _():
            for which in range(2):
                edge_copy(which, h).start()

    def wait_sends(h):
        for j in range(4):
            @pl.when(exists(offsets[j]))
            def _():
                for which in range(2):
                    kv_copy(j, which, h).wait_send()

        @pl.when(me == n - 1)
        def _():
            for which in range(2):
                edge_copy(which, h).wait_send()

    def wait_recvs(h):
        for j, there in enumerate((me >= 1, me >= 2, me <= n - 2, me <= n - 2)):
            @pl.when(there)
            def _():
                for which in range(2):
                    kv_copy(j, which, h).wait_recv()

    def own_copy(b, which, h):
        return pltpu.make_async_copy(
            part((k_hbm, v_hbm)[which], b * half, h), kv.at[b, which, h], own_sem.at[b, which, h])

    for j in range(4):
        @pl.when(exists(offsets[j]))
        def _():
            seg_copy(j).start()
    start_sends(0)
    start_sends(1)
    q_copy = pltpu.make_async_copy(q_hbm, q_vm, q_sem)
    q_copy.start()
    for h in range(kv_heads):
        for b in range(2):
            for which in range(2):
                own_copy(b, which, h).start()

    for slot, missing in ((FP1, me < 1), (FP2, me < 2)):
        @pl.when(missing)
        def _():
            kv[slot] = jnp.zeros(kv.shape[1:], kv.dtype)
            segs[slot - FP1] = jnp.full(segs.shape[1:], -1, segs.dtype)

    segs[4] = seg_ref[...]
    for j in range(4):
        there = exists(-offsets[j])

        @pl.when(there)
        def _():
            seg_copy(j).wait_recv()

    last = me == n - 1
    second = me == n - 2
    seg_places = (
        ((1, 0), (0, 0), (4, 0)),
        (
            (jnp.where(last, 0, jnp.where(second, 2, 3)), jnp.where(last | second, 0, rows_seg)),
            (jnp.where(last, 4, 2), jnp.where(last, 0, rows_seg)),
            (4, rows_seg),
        ),
    )
    for b in range(2):
        band = []
        for slot, row in seg_places[b]:
            for c in range(rows_seg):
                band.append(segs[slot, pl.ds(row + c, 1), :])
        for c in range(rows_seg):
            own = band[2 * rows_seg + c]
            own_col = jnp.transpose(jnp.broadcast_to(own, (LANES, LANES)))
            count = jnp.zeros((LANES, LANES), jnp.float32)
            for keys in band:
                count = count + jnp.where(keys < own_col, 1.0, 0.0)
            first = jnp.sum(count, axis=1, keepdims=True).astype(jnp.int32)
            row_of = lax.broadcasted_iota(jnp.int32, (LANES, LANES), 0) + (c * LANES + 1)
            lo[b, pl.ds(c * LANES, LANES), :] = jnp.maximum(jnp.broadcast_to(first, (LANES, LANES)), row_of)

    q_copy.wait()

    def out_copy(h):
        cols = pl.ds(pl.multiple_of(h * groups * HEAD_DIM, HEAD_DIM), groups * HEAD_DIM)
        return pltpu.make_async_copy(o_vm.at[:, cols], o_hbm.at[:, cols], o_sem.at[h])

    def attend(h, b, g):
        older1 = jnp.where(b == 0, FP1, jnp.where(last, OWN_F, BN1))
        older2 = jnp.where(b == 0, FP2, jnp.where(last, FP1, BN2))
        col = pl.multiple_of((h * groups + g) * HEAD_DIM, HEAD_DIM)
        for t in range(half // TILE):
            row = pl.multiple_of(b * half + t * TILE, TILE)
            q = q_vm[pl.ds(row, TILE), pl.ds(col, HEAD_DIM)]
            low = lo[b, pl.ds(t * TILE, TILE), 0:1]
            pieces = (
                (older2, t * TILE, half - t * TILE, t * TILE),
                (older1, 0, half, half),
                (b, 0, (t + 1) * TILE, 2 * half),
            )
            scores = []
            for p, (slot, k0, kn, base) in enumerate(pieces):
                k = kv[slot, 0, h, pl.ds(k0, kn), :]
                s = lax.dot_general(q, k, (((1,), (1,)), ((), ())), preferred_element_type=jnp.float32)
                key_at = lax.broadcasted_iota(jnp.int32, (TILE, kn), 1) + base
                seen = key_at >= low
                if p == 2:
                    row_at = lax.broadcasted_iota(jnp.int32, (TILE, kn), 0) + (2 * half + t * TILE)
                    seen = seen & (key_at <= row_at)
                scores.append(jnp.where(seen, s * SCALE2, NEG))
            top = functools.reduce(jnp.maximum, [jnp.max(s, axis=1, keepdims=True) for s in scores])
            acc = None
            for s, (slot, k0, kn, base) in zip(scores, pieces):
                w = jnp.exp2(s - top).astype(jnp.bfloat16)
                v = kv[slot, 1, h, pl.ds(k0, kn), :]
                v = jnp.concatenate([v, jnp.ones((kn, LANES), jnp.bfloat16)], axis=1)
                d = lax.dot_general(w, v, (((1,), (0,)), ((), ())), preferred_element_type=jnp.float32)
                acc = d if acc is None else acc + d
            o_vm[pl.ds(row, TILE), pl.ds(col, HEAD_DIM)] = (
                acc[:, :HEAD_DIM] / acc[:, HEAD_DIM:]).astype(o_vm.dtype)

    def head_step(h, carry):
        for b in range(2):
            for which in range(2):
                own_copy(b, which, h).wait()
        wait_recvs(h)

        @pl.when(h + 2 < kv_heads)
        def _():
            start_sends(h + 2)

        def one(i, c):
            attend(h, i // groups, i % groups)
            return c

        lax.fori_loop(0, 2 * groups, one, 0)
        out_copy(h).start()
        return carry

    lax.fori_loop(0, kv_heads, head_step, 0)

    for j in range(4):
        @pl.when(exists(offsets[j]))
        def _():
            seg_copy(j).wait_send()

    def finish(h, carry):
        wait_sends(h)
        out_copy(h).wait()
        return carry

    lax.fori_loop(0, kv_heads, finish, 0)


def body(queries, key_states, value_states, segment_ids):
    rows, q_cols = queries.shape
    half = rows // 2
    kv_heads = key_states.shape[1] // HEAD_DIM
    groups = q_cols // key_states.shape[1]
    n = lax.axis_size("seq")
    seg_tile = segment_ids.reshape(rows // LANES, LANES)
    anywhere = pl.BlockSpec(memory_space=pl.ANY)
    flops = 4 * rows * q_cols * 5 * TILE
    return pl.pallas_call(
        functools.partial(kernel, n, kv_heads, groups),
        out_shape=jax.ShapeDtypeStruct((rows, q_cols), jnp.bfloat16),
        in_specs=[anywhere, anywhere, anywhere, pl.BlockSpec(memory_space=pltpu.VMEM)],
        out_specs=anywhere,
        scratch_shapes=[
            pltpu.VMEM((6, 2, kv_heads, half, HEAD_DIM), jnp.bfloat16),
            pltpu.VMEM((rows, q_cols), jnp.bfloat16),
            pltpu.VMEM((rows, q_cols), jnp.bfloat16),
            pltpu.VMEM((5, rows // LANES, LANES), jnp.int32),
            pltpu.VMEM((2, half, LANES), jnp.int32),
            pltpu.SemaphoreType.DMA((5, 2, kv_heads)),
            pltpu.SemaphoreType.DMA((4, 2, kv_heads)),
            pltpu.SemaphoreType.DMA((4,)),
            pltpu.SemaphoreType.DMA((4,)),
            pltpu.SemaphoreType.DMA((2, 2, kv_heads)),
            pltpu.SemaphoreType.DMA,
            pltpu.SemaphoreType.DMA((kv_heads,)),
        ],
        compiler_params=pltpu.CompilerParams(
            collective_id=0, has_side_effects=True, vmem_limit_bytes=48 * 1024 * 1024),
        cost_estimate=pl.CostEstimate(
            flops=flops, bytes_accessed=6 * rows * q_cols, transcendentals=8 * rows * 5 * TILE),
    )(queries, key_states, value_states, seg_tile)


def solution(mesh):
    in_specs = (
        P(("grp", "seq"), "head"),
        P(("grp", "seq"), "head"),
        P(("grp", "seq"), "head"),
        P(("grp", "seq")),
    )
    out_specs = P(("grp", "seq"), "head")
    return jax.shard_map(body, mesh=mesh, in_specs=in_specs, out_specs=out_specs, check_vma=False)
```

time: 185 us -> 81.4 us (0.44)
  the two profiles are of different devices: /device:TPU:0 before, /device:TPU:24 now
where the time goes in v1:
time: 81.4 us; the launch traced here: 81.2 us
  Pallas kernels  76.7 us (94%)
  local copies, waits for them, and re-layouts  4.46 us (5%)
    pallas_call x1, Pallas kernels, body(): pl.pallas_call(functools.partial(kernel, n, kv_heads, groups), out_shape=...  76.7 us
    unnamed x7, local copies, waits for them, and re-layouts  4.46 us

profile of v1, /device:TPU:24, one launch (start us, length us, event | category | flops | bytes accessed | tf_op | source)
XLA Modules:
  0.0 81.2 jit_solution(7932161735763440359)
XLA Ops:
  0.0 0.0 copy-start
  0.0 1.2 %copy-done = bf16[1024,512]{1,0:T(8,128)(2,1)S(1)} copy-done((bf16[1024,512]{1,0:T(8,128)(2,1)S(1)}, bf16[1024,512]{1,0:T(8,128)(2,1)}, u32[]{:S(2)}) %copy-start) | copy-done | bytes 1048600
  1.2 0.0 copy-start.1
  1.2 1.2 %copy-done.1 = bf16[1024,512]{1,0:T(8,128)(2,1)S(1)} copy-done((bf16[1024,512]{1,0:T(8,128)(2,1)S(1)}, bf16[1024,512]{1,0:T(8,128)(2,1)}, u32[]{:S(2)}) %copy-start.1) | copy-done | bytes 1048600
  2.5 0.0 copy-start.2
  2.5 0.7 copy-done.2
  3.1 76.7 %shard_map.46 = bf16[1024,1024]{1,0:T(8,128)(2,1)S(1)} custom-call(bf16[1024,1024]{1,0:T(8,128)(2,1)} %q_hbm.1, bf16[1024,512]{1,0:T(8,128)(2,1)S(1)} %copy-done, bf16[1024,512]{1,0:T(8,128)(2,1)S(1)} %copy-done.1, s32[8,128]{1,0:T(8,128)S(1)} %bitcast.1), custom_call_target="tpu_custom_call" | custom-call | flops 5368709120 | bytes 6291456 | tf_op jit(solution)/shard_map/pallas_call | solution.py:234
  79.9 1.3 %copy.6 = bf16[1024,1024]{1,0:T(8,128)(2,1)} copy(bf16[1024,1024]{1,0:T(8,128)(2,1)S(1)} %shard_map.46) | data formatting | bytes 4194304
Async XLA Ops:
  0.0 1.2 %copy-start = (bf16[1024,512]{1,0:T(8,128)(2,1)S(1)}, bf16[1024,512]{1,0:T(8,128)(2,1)}, u32[]{:S(2)}) copy-start(bf16[1024,512]{1,0:T(8,128)(2,1)} %k_hbm.1) | copy-start | bytes 3145732
  1.2 1.2 %copy-start.1 = (bf16[1024,512]{1,0:T(8,128)(2,1)S(1)}, bf16[1024,512]{1,0:T(8,128)(2,1)}, u32[]{:S(2)}) copy-start(bf16[1024,512]{1,0:T(8,128)(2,1)} %v_hbm.1) | copy-start | bytes 3145732
  2.5 0.7 copy-start.2

commit v2 on v1

--- a/solution.py
+++ b/solution.py
@@ -16,10 +16,10 @@
 SCALE2 = (168.0 ** (-0.5)) * 1.4426950408889634
 NEG = -1e30
 
-OWN_F, OWN_B, FP1, FP2, BN1, BN2 = range(6)
-
-
-def kernel(n, kv_heads, groups, q_hbm, k_hbm, v_hbm, seg_ref, o_hbm,
+OWN_F, OWN_B, FP1, FP2, BN1, BN2, RELAY = range(7)
+
+
+def kernel(n, relay, kv_heads, groups, q_hbm, k_hbm, v_hbm, seg_ref, o_hbm,
            kv, q_vm, o_vm, segs, lo,
            send_sem, recv_sem, seg_send, seg_recv, own_sem, q_sem, o_sem):
     me = lax.axis_index("seq")
@@ -48,50 +48,56 @@
     def part(ref, row, h):
         return ref.at[pl.ds(row, half), pl.ds(pl.multiple_of(h * HEAD_DIM, HEAD_DIM), HEAD_DIM)]
 
-    def kv_copy(j, which, h, off=None, row=None):
-        off = offsets[j] if off is None else off
-        row = (0 if j < 2 else half) if row is None else row
-        return pltpu.make_async_remote_copy(
-            src_ref=part((k_hbm, v_hbm)[which], row, h), dst_ref=kv.at[slots[j], which, h],
+    def kv_copy(j, which, h):
+        return pltpu.make_async_remote_copy(
+            src_ref=part((k_hbm, v_hbm)[which], 0 if j < 2 else half, h), dst_ref=kv.at[slots[j], which, h],
             send_sem=send_sem.at[j, which, h], recv_sem=recv_sem.at[j, which, h],
-            device_id={"seq": me + off}, device_id_type=MESH)
-
-    def edge_copy(which, h):
-        return pltpu.make_async_remote_copy(
-            src_ref=part((k_hbm, v_hbm)[which], 0, h), dst_ref=kv.at[BN2, which, h],
-            send_sem=send_sem.at[4, which, h], recv_sem=recv_sem.at[3, which, h],
+            device_id={"seq": me + offsets[j]}, device_id_type=MESH)
+
+    def down_copy(which, h):
+        return pltpu.make_async_remote_copy(
+            src_ref=part((k_hbm, v_hbm)[which], 0, h), dst_ref=kv.at[RELAY, which, h],
+            send_sem=send_sem.at[4, which, h], recv_sem=recv_sem.at[4, which, h],
             device_id={"seq": me - 1}, device_id_type=MESH)
 
-    def start_sends(h):
+    def relay_copy(which, h):
+        return pltpu.make_async_remote_copy(
+            src_ref=kv.at[RELAY, which, h], dst_ref=kv.at[FP1, which, h],
+            send_sem=send_sem.at[5, which, h], recv_sem=recv_sem.at[0, which, h],
+            device_id={"seq": me + 2}, device_id_type=MESH)
+
+    odd = me % 2 == 1
+    if relay:
+        sends_down, gets_down = odd, jnp.logical_not(odd)
+        relays = jnp.logical_not(odd) & (me + 2 < n)
+        sends_up = jnp.logical_not(odd)
+    else:
+        sends_down, gets_down = me == n - 1, me == n - 2
+        relays = None
+        sends_up = me + 1 < n
+    sends = (sends_up, exists(2), exists(-1), exists(-2))
+
+    def each(condition, action):
+        @pl.when(condition)
+        def _():
+            for which in range(2):
+                action(which)
+
+    def start_front(h):
+        each(sends_down, lambda w: down_copy(w, h).start())
+        for j in (0, 1):
+            each(sends[j], lambda w: kv_copy(j, w, h).start())
+
+    def start_back(h):
+        for j in (2, 3):
+            each(sends[j], lambda w: kv_copy(j, w, h).start())
+
+    def wait_sends(h):
+        each(sends_down, lambda w: down_copy(w, h).wait_send())
         for j in range(4):
-            @pl.when(exists(offsets[j]))
-            def _():
-                for which in range(2):
-                    kv_copy(j, which, h).start()
-
-        @pl.when(me == n - 1)
-        def _():
-            for which in range(2):
-                edge_copy(which, h).start()
-
-    def wait_sends(h):
-        for j in range(4):
-            @pl.when(exists(offsets[j]))
-            def _():
-                for which in range(2):
-                    kv_copy(j, which, h).wait_send()
-
-        @pl.when(me == n - 1)
-        def _():
-            for which in range(2):
-                edge_copy(which, h).wait_send()
-
-    def wait_recvs(h):
-        for j, there in enumerate((me >= 1, me >= 2, me <= n - 2, me <= n - 2)):
-            @pl.when(there)
-            def _():
-                for which in range(2):
-                    kv_copy(j, which, h).wait_recv()
+            each(sends[j], lambda w: kv_copy(j, w, h).wait_send())
+        if relay:
+            each(relays, lambda w: relay_copy(w, h).wait_send())
 
     def own_copy(b, which, h):
         return pltpu.make_async_copy(
@@ -101,8 +107,9 @@
         @pl.when(exists(offsets[j]))
         def _():
             seg_copy(j).start()
-    start_sends(0)
-    start_sends(1)
+    for h in range(min(2, kv_heads)):
+        start_front(h)
+        start_back(h)
     q_copy = pltpu.make_async_copy(q_hbm, q_vm, q_sem)
     q_copy.start()
     for h in range(kv_heads):
@@ -157,7 +164,7 @@
 
     def attend(h, b, g):
         older1 = jnp.where(b == 0, FP1, jnp.where(last, OWN_F, BN1))
-        older2 = jnp.where(b == 0, FP2, jnp.where(last, FP1, BN2))
+        older2 = jnp.where(b == 0, FP2, jnp.where(last, FP1, jnp.where(second, RELAY, BN2)))
         col = pl.multiple_of((h * groups + g) * HEAD_DIM, HEAD_DIM)
         for t in range(half // TILE):
             row = pl.multiple_of(b * half + t * TILE, TILE)
@@ -190,20 +197,30 @@
                 acc[:, :HEAD_DIM] / acc[:, HEAD_DIM:]).astype(o_vm.dtype)
 
     def head_step(h, carry):
+        each(gets_down, lambda w: down_copy(w, h).wait_recv())
+        if relay:
+            each(relays, lambda w: relay_copy(w, h).start())
         for b in range(2):
             for which in range(2):
                 own_copy(b, which, h).wait()
-        wait_recvs(h)
+        each(me >= 1, lambda w: kv_copy(0, w, h).wait_recv())
+        each(me >= 2, lambda w: kv_copy(1, w, h).wait_recv())
 
         @pl.when(h + 2 < kv_heads)
         def _():
-            start_sends(h + 2)
-
-        def one(i, c):
-            attend(h, i // groups, i % groups)
-            return c
-
-        lax.fori_loop(0, 2 * groups, one, 0)
+            start_front(h + 2)
+
+        for g in range(groups):
+            attend(h, 0, g)
+        each(me <= n - 2, lambda w: kv_copy(2, w, h).wait_recv())
+        each(me <= n - 3, lambda w: kv_copy(3, w, h).wait_recv())
+
+        @pl.when(h + 2 < kv_heads)
+        def _():
+            start_back(h + 2)
+
+        for g in range(groups):
+            attend(h, 1, g)
         out_copy(h).start()
         return carry
 
@@ -228,22 +245,23 @@
     kv_heads = key_states.shape[1] // HEAD_DIM
     groups = q_cols // key_states.shape[1]
     n = lax.axis_size("seq")
+    relay = n == 8
     seg_tile = segment_ids.reshape(rows // LANES, LANES)
     anywhere = pl.BlockSpec(memory_space=pl.ANY)
     flops = 4 * rows * q_cols * 5 * TILE
     return pl.pallas_call(
-        functools.partial(kernel, n, kv_heads, groups),
+        functools.partial(kernel, n, relay, kv_heads, groups),
         out_shape=jax.ShapeDtypeStruct((rows, q_cols), jnp.bfloat16),
         in_specs=[anywhere, anywhere, anywhere, pl.BlockSpec(memory_space=pltpu.VMEM)],
         out_specs=anywhere,
         scratch_shapes=[
-            pltpu.VMEM((6, 2, kv_heads, half, HEAD_DIM), jnp.bfloat16),
+            pltpu.VMEM((7, 2, kv_heads, half, HEAD_DIM), jnp.bfloat16),
             pltpu.VMEM((rows, q_cols), jnp.bfloat16),
             pltpu.VMEM((rows, q_cols), jnp.bfloat16),
             pltpu.VMEM((5, rows // LANES, LANES), jnp.int32),
             pltpu.VMEM((2, half, LANES), jnp.int32),
+            pltpu.SemaphoreType.DMA((6, 2, kv_heads)),
             pltpu.SemaphoreType.DMA((5, 2, kv_heads)),
-            pltpu.SemaphoreType.DMA((4, 2, kv_heads)),
             pltpu.SemaphoreType.DMA((4,)),
             pltpu.SemaphoreType.DMA((4,)),
             pltpu.SemaphoreType.DMA((2, 2, kv_heads)),
@@ -251,7 +269,7 @@
             pltpu.SemaphoreType.DMA((kv_heads,)),
         ],
         compiler_params=pltpu.CompilerParams(
-            collective_id=0, has_side_effects=True, vmem_limit_bytes=48 * 1024 * 1024),
+            collective_id=0, has_side_effects=True, vmem_limit_bytes=60 * 1024 * 1024),
         cost_estimate=pl.CostEstimate(
             flops=flops, bytes_accessed=6 * rows * q_cols, transcendentals=8 * rows * 5 * TILE),
     )(queries, key_states, value_states, seg_tile)

time: 81.4 us -> 62.9 us (0.77)
  Pallas kernels: 76.7 us -> 59.7 us
  local copies, waits for them, and re-layouts: 4.46 us -> 3.08 us
    pallas_call x1, Pallas kernels: 76.7 us -> 59.7 us  [body(): pl.pallas_call(functools.partial(kernel, n, relay, kv_heads, groups), out...]
    unnamed x7 -> x1, local copies, waits for them, and re-layouts: 4.46 us -> 3.08 us
where the time goes in v2:
time: 62.9 us; the launch traced here: 62.8 us
  Pallas kernels  59.7 us (95%)
  local copies, waits for them, and re-layouts  3.08 us (5%)
    pallas_call x1, Pallas kernels, body(): pl.pallas_call(functools.partial(kernel, n, relay, kv_heads, groups), out...  59.7 us
    unnamed x1, local copies, waits for them, and re-layouts  3.08 us

profile of v2, /device:TPU:24, one launch (start us, length us, event | category | flops | bytes accessed | tf_op | source)
XLA Modules:
  0.0 62.8 jit_solution(9305674567259515583)
XLA Ops:
  0.0 59.7 %shard_map.46 = bf16[1024,1024]{1,0:T(8,128)(2,1)} custom-call(bf16[1024,1024]{1,0:T(8,128)(2,1)} %q_hbm.1, bf16[1024,512]{1,0:T(8,128)(2,1)} %k_hbm.1, bf16[1024,512]{1,0:T(8,128)(2,1)} %v_hbm.1, s32[8,128]{1,0:T(8,128)} %bitcast.1), custom_call_target="tpu_custom_call" | custom-call | flops 5368709120 | bytes 6291456 | tf_op jit(solution)/shard_map/pallas_call | solution.py:252
  59.7 3.1 %copy.6 = bf16[1024,1024]{1,0:T(8,128)(2,1)} copy(bf16[1024,1024]{1,0:T(8,128)(2,1)} %shard_map.46) | data formatting | bytes 4194304

commit v3 on v2

--- a/solution.py
+++ b/solution.py
@@ -19,9 +19,9 @@
 OWN_F, OWN_B, FP1, FP2, BN1, BN2, RELAY = range(7)
 
 
-def kernel(n, relay, kv_heads, groups, q_hbm, k_hbm, v_hbm, seg_ref, o_hbm,
-           kv, q_vm, o_vm, segs, lo,
-           send_sem, recv_sem, seg_send, seg_recv, own_sem, q_sem, o_sem):
+def kernel(n, relay, kv_heads, groups, q_hbm, k_hbm, v_hbm, seg_ref, o_vm,
+           kv, q_vm, segs, lo,
+           send_sem, recv_sem, seg_send, seg_recv, own_sem, q_sem):
     me = lax.axis_index("seq")
     half = q_vm.shape[0] // 2
     rows_seg = half // LANES
@@ -157,10 +157,6 @@
             lo[b, pl.ds(c * LANES, LANES), :] = jnp.maximum(jnp.broadcast_to(first, (LANES, LANES)), row_of)
 
     q_copy.wait()
-
-    def out_copy(h):
-        cols = pl.ds(pl.multiple_of(h * groups * HEAD_DIM, HEAD_DIM), groups * HEAD_DIM)
-        return pltpu.make_async_copy(o_vm.at[:, cols], o_hbm.at[:, cols], o_sem.at[h])
 
     def attend(h, b, g):
         older1 = jnp.where(b == 0, FP1, jnp.where(last, OWN_F, BN1))
@@ -196,10 +192,12 @@
             o_vm[pl.ds(row, TILE), pl.ds(col, HEAD_DIM)] = (
                 acc[:, :HEAD_DIM] / acc[:, HEAD_DIM:]).astype(o_vm.dtype)
 
-    def head_step(h, carry):
+    def pass_on(h):
         each(gets_down, lambda w: down_copy(w, h).wait_recv())
         if relay:
             each(relays, lambda w: relay_copy(w, h).start())
+
+    def head_step(h, carry):
         for b in range(2):
             for which in range(2):
                 own_copy(b, which, h).wait()
@@ -219,11 +217,15 @@
         def _():
             start_back(h + 2)
 
+        @pl.when(h + 1 < kv_heads)
+        def _():
+            pass_on(h + 1)
+
         for g in range(groups):
             attend(h, 1, g)
-        out_copy(h).start()
         return carry
 
+    pass_on(0)
     lax.fori_loop(0, kv_heads, head_step, 0)
 
     for j in range(4):
@@ -233,7 +235,6 @@
 
     def finish(h, carry):
         wait_sends(h)
-        out_copy(h).wait()
         return carry
 
     lax.fori_loop(0, kv_heads, finish, 0)
@@ -251,12 +252,11 @@
     flops = 4 * rows * q_cols * 5 * TILE
     return pl.pallas_call(
         functools.partial(kernel, n, relay, kv_heads, groups),
-        out_shape=jax.ShapeDtypeStruct((rows, q_cols), jnp.bfloat16),
+        out_shape=pltpu.VMEM((rows, q_cols), jnp.bfloat16),
         in_specs=[anywhere, anywhere, anywhere, pl.BlockSpec(memory_space=pltpu.VMEM)],
-        out_specs=anywhere,
+        out_specs=pl.BlockSpec(memory_space=pltpu.VMEM),
         scratch_shapes=[
             pltpu.VMEM((7, 2, kv_heads, half, HEAD_DIM), jnp.bfloat16),
-            pltpu.VMEM((rows, q_cols), jnp.bfloat16),
             pltpu.VMEM((rows, q_cols), jnp.bfloat16),
             pltpu.VMEM((5, rows // LANES, LANES), jnp.int32),
             pltpu.VMEM((2, half, LANES), jnp.int32),
@@ -266,7 +266,6 @@
             pltpu.SemaphoreType.DMA((4,)),
             pltpu.SemaphoreType.DMA((2, 2, kv_heads)),
             pltpu.SemaphoreType.DMA,
-            pltpu.SemaphoreType.DMA((kv_heads,)),
         ],
         compiler_params=pltpu.CompilerParams(
             collective_id=0, has_side_effects=True, vmem_limit_bytes=60 * 1024 * 1024),

time: 62.9 us -> 58 us (0.922)
  Pallas kernels: 59.7 us -> 55.9 us
  local copies, waits for them, and re-layouts: 3.08 us -> 1.32 us
    pallas_call x1, Pallas kernels: 59.7 us -> 55.9 us  [body(): pl.pallas_call(functools.partial(kernel, n, relay, kv_heads, groups), out...]
    unnamed x1, local copies, waits for them, and re-layouts: 3.08 us -> 1.32 us
where the time goes in v3:
time: 58 us; the launch traced here: 57.3 us
  Pallas kernels  55.9 us (96%)
  local copies, waits for them, and re-layouts  1.32 us (2%)
    pallas_call x1, Pallas kernels, body(): pl.pallas_call(functools.partial(kernel, n, relay, kv_heads, groups), out...  55.9 us
    unnamed x1, local copies, waits for them, and re-layouts  1.32 us

profile of v3, /device:TPU:24, one launch (start us, length us, event | category | flops | bytes accessed | tf_op | source)
XLA Modules:
  0.0 57.3 jit_solution(18415802276141571426)
XLA Ops:
  0.0 55.9 %shard_map.46 = bf16[1024,1024]{1,0:T(8,128)(2,1)S(1)} custom-call(bf16[1024,1024]{1,0:T(8,128)(2,1)} %q_hbm.1, bf16[1024,512]{1,0:T(8,128)(2,1)} %k_hbm.1, bf16[1024,512]{1,0:T(8,128)(2,1)} %v_hbm.1, s32[8,128]{1,0:T(8,128)} %bitcast.1), custom_call_target="tpu_custom_call" | custom-call | flops 5368709120 | bytes 6291456 | tf_op jit(solution)/shard_map/pallas_call | solution.py:253
  56.0 1.3 %copy.6 = bf16[1024,1024]{1,0:T(8,128)(2,1)} copy(bf16[1024,1024]{1,0:T(8,128)(2,1)S(1)} %shard_map.46) | data formatting | bytes 4194304
